TPU v7x, 32 devices: a whole 2x2x4 slice. The times are simulated.
32 devices in a mesh: parts: 2 (over x), tensor: 16 (over z, y, core).
Axes of the slice: x: 2, y: 2, z: 4, core: 2. Of those that a mesh axis runs over, the one named last changes fastest.
Arguments:
- tokens: bfloat16 [512, 8192], P(('parts', 'tensor')), parts along dimension 0, may hold values from -6 to 6
- out_grad: bfloat16 [512, 8192], P(('parts', 'tensor')), parts along dimension 0, may hold values from -6 to 6
- gate_weight: bfloat16 [8192, 20480], P(None, 'tensor'), may hold values from -0.0625 to 0.0625
- down_weight: bfloat16 [20480, 8192], P('tensor'), may hold values from -0.0390625 to 0.0390625
- proj_in: bfloat16 [8192, 64], replicated, may hold values from -0.0625 to 0.0625
- proj_out: bfloat16 [20480, 64], P('tensor'), may hold values from -0.0390625 to 0.0390625
- lengths: int32 [8], P('parts'), parts along dimension 0, may hold values from 1 to 128, 256 in all
- query_features: float32 [1024, 4096], P(None, 'tensor'), may hold values from -0.1 to 0.1
Outputs:
- train_features: float32 [8, 4096], P('parts', 'tensor'), parts along dimension 0
- scores: float32 [8, 1024], P('parts'), parts along dimension 0
There are 2 independent parts, one for each index of `parts`. A program takes and returns all parts, laid end to end along the dimension named above; an argument that names none is the same for every part. Nothing has to cross between parts.
Inputs may be any that keep to these rules, and one draw needn't show every extreme that they name: The lengths sum to 256, and the largest is exactly 128.
All inputs are finite; a program needn't handle non-finite values.
Results may differ from a plain program's by a relative error of at most 0.0031.
Values may be sent and summed in bfloat16 or wider, within the bound.
A program may use at most 192 MiB of HBM per device.

v0:
```python
import jax
import jax.numpy as jnp
from jax import lax
from jax.sharding import PartitionSpec as P


def kron_features(member, proj_x, proj_g):
    rows = proj_x.shape[0]
    width = proj_x.shape[1]
    count = member.shape[1]
    weighted = (member[:, :, None] * proj_x[:, None, :]).reshape(rows, count * width)
    feats = lax.dot_general(
        weighted, proj_g, (((0,), (0,)), ((), ())), precision=lax.Precision.HIGHEST
    )
    return feats.reshape(count, width * proj_g.shape[1])


def membership(lengths, rows):
    ends = jnp.cumsum(lengths)
    starts = ends - lengths
    place = jnp.arange(rows, dtype=jnp.int32)[:, None]
    inside = (place >= starts[None, :]) & (place < ends[None, :])
    return inside.astype(jnp.float32)


def pair_scores(feats, queries):
    return lax.dot_general(
        feats, queries, (((1,), (1,)), ((), ())), precision=lax.Precision.HIGHEST
    )


def on_device(
    tokens, out_grad, gate_weight, down_weight, proj_in, proj_out, lengths, query_features
):
    whole_x, whole_dy = (
        lax.all_gather(tokens, "tensor", axis=0, tiled=True),
        lax.all_gather(out_grad, "tensor", axis=0, tiled=True),
    )
    gate = jnp.dot(whole_x, gate_weight, preferred_element_type=jnp.float32)
    grad_hidden = lax.dot_general(
        whole_dy, down_weight, (((1,), (1,)), ((), ())), preferred_element_type=jnp.float32
    )
    grad_up = (grad_hidden * jax.nn.silu(gate)).astype(jnp.bfloat16)
    proj_x = jnp.dot(whole_x, proj_in, preferred_element_type=jnp.float32)
    part_g = jnp.dot(grad_up, proj_out, preferred_element_type=jnp.float32)
    member = membership(lengths, whole_x.shape[0])
    columns = query_features.shape[1]
    full_g = lax.psum(part_g, "tensor")
    feats = kron_features(member, proj_x, full_g)
    every_query = lax.all_gather(query_features, "tensor", axis=1, tiled=True)
    scores = pair_scores(feats, every_query)
    own_feats = lax.dynamic_slice_in_dim(feats, lax.axis_index("tensor") * columns, columns, 1)
    return (own_feats, scores)


def solution(mesh):
    placed = (
        P(("parts", "tensor"), None),
        P(("parts", "tensor"), None),
        P(None, "tensor"),
        P("tensor", None),
        P(),
        P("tensor", None),
        P("parts"),
        P(None, "tensor"),
    )
    return jax.shard_map(
        on_device,
        mesh=mesh,
        in_specs=placed,
        out_specs=(P("parts", "tensor"), P("parts", None)),
        check_vma=False,
    )
```

profile of v0, /device:TPU:0, one launch (start us, length us, event | category | flops | bytes accessed | tf_op | source)
XLA Modules:
  0.0 371.7 jit_solution(2041721907225374325)
XLA Ops:
  7.2 0.0 copy-start
  7.2 0.0 all-gather.4.cloned.1.call-start
  7.2 0.7 all-gather.4.cloned.1.call-update
  7.9 0.0 all-gather.6.cloned.1.call-start
  8.0 0.7 all-gather.6.cloned.1.call-update
  8.7 0.0 copy-start.1
  8.7 0.0 all-reduce.2.cloned.1.call-start
  8.7 54.7 %all-gather.4.cloned.1.call-done = bf16[256,8192]{1,0:T(8,128)(2,1)} async-done(((bf16[16,8192]{1,0:T(8,128)(2,1)}), bf16[256,8192]{1,0:T(8,128)(2,1)}) %all-gather.4.cloned.1.call-update) | async-done | bytes 4194320 | tf_op jit(solution)/shard_map/all_gather | solution.py:36
  63.5 12.3 %fusion.7 = f32[256,1280]{1,0:T(8,128)S(1)} fusion(bf16[256,8192]{1,0:T(8,128)(2,1)} %all-gather.4.cloned.1.call-done, bf16[8192,1280]{1,0:T(8,128)(2,1)} %param.10), kind=kOutput, calls=%fused_computation.13 | convolution fusion | flops 5368709120 | bytes 26476544 | tf_op jit(solution)/shard_map/dot_general | solution.py:39
  75.7 0.0 copy-start.2
  75.7 39.0 %all-gather.6.cloned.1.call-done = bf16[256,8192]{1,0:T(8,128)(2,1)} async-done(((bf16[16,8192]{1,0:T(8,128)(2,1)}), bf16[256,8192]{1,0:T(8,128)(2,1)}) %all-gather.6.cloned.1.call-update) | async-done | bytes 4194320 | tf_op jit(solution)/shard_map/all_gather | solution.py:37
  114.7 0.0 copy-done.1
  114.7 13.2 %fusion.1 = f32[256,64]{1,0:T(8,128)} fusion(bf16[1280,64]{0,1:T(8,128)(2,1)S(1)} %copy-done.1, bf16[256,8192]{1,0:T(8,128)(2,1)} %all-gather.6.cloned.1.call-done, bf16[1280,8192]{1,0:T(8,128)(2,1)} %param.11, f32[256,1280]{1,0:T(8,128)S(1)} %fusion.7), kind=kOutput, calls=%fused_computation.2 | convolution fusion | flops 5412618240 | bytes 26705920 | tf_op jit(solution)/shard_map/dot_general | solution.py:45
  127.9 0.0 all-reduce.2.cloned.1.call-update
  128.0 0.2 all-gather.8.cloned.1.call-start
  128.2 0.3 all-gather.8.cloned.1.call-update
  128.5 0.0 copy-done.2
  128.5 0.2 reduce-window.8
  128.7 0.1 fusion.4
  128.8 0.0 copy-done
  128.8 3.6 fusion.6
  132.4 81.0 %all-reduce.2.cloned.1.call-done = f32[256,64]{1,0:T(8,128)} async-done(((f32[256,64]{1,0:T(8,128)}), f32[256,64]{1,0:T(8,128)}) %all-reduce.2.cloned.1.call-update) | async-done | bytes 65552 | tf_op jit(solution)/shard_map/psum | solution.py:48
  213.5 1.3 fusion.8
  214.8 0.1 reshape.76
  214.9 0.6 constant_dynamic-slice_fusion
  215.5 132.0 %all-gather.8.cloned.1.call-done = f32[1024,4096]{1,0:T(8,128)} async-done(((f32[1024,256]{1,0:T(8,128)}), f32[1024,4096]{1,0:T(8,128)}) %all-gather.8.cloned.1.call-update) | async-done | bytes 16777232 | tf_op jit(solution)/shard_map/all_gather | solution.py:50
  347.5 17.7 %fusion.9 = f32[4,1024]{1,0:T(4,128)} fusion(f32[4,4096]{1,0:T(4,128)S(1)} %reshape.76, f32[1024,4096]{1,0:T(8,128)} %all-gather.8.cloned.1.call-done), kind=kOutput, calls=%fused_computation.15 | convolution fusion | flops 201326592 | bytes 16859136 | tf_op jit(solution)/shard_map/dot_general | solution.py:27
  (2 shorter events, 0.0 us)
Async XLA Ops:
  7.2 121.6 %copy-start = (bf16[8192,64]{0,1:T(8,128)(2,1)S(1)}, bf16[8192,64]{0,1:T(8,128)(2,1)}, u32[]{:S(2)}) copy-start(bf16[8192,64]{0,1:T(8,128)(2,1)} %param.12) | copy-start | bytes 3145732
  7.2 56.3 %all-gather.4.cloned.1.call-start = ((), (), s32[]{:S(2)}) async-start(), calls=%async_computation | async-start | bytes 4456448 | tf_op jit(solution)/shard_map/all_gather | solution.py:36
  7.9 106.8 %all-gather.6.cloned.1.call-start = ((), (), s32[]{:S(2)}) async-start(), calls=%async_computation.1 | async-start | bytes 4456448 | tf_op jit(solution)/shard_map/all_gather | solution.py:37
  8.7 106.1 %copy-start.1 = (bf16[1280,64]{0,1:T(8,128)(2,1)S(1)}, bf16[1280,64]{0,1:T(8,128)(2,1)}, u32[]{:S(2)}) copy-start(bf16[1280,64]{0,1:T(8,128)(2,1)} %param.13) | copy-start | bytes 491524
  8.7 204.8 %all-reduce.2.cloned.1.call-start = ((), (), s32[]{:S(2)}) async-start(), calls=%async_computation.2 | async-start | bytes 262144 | tf_op jit(solution)/shard_map/psum | solution.py:48
  75.7 52.8 %copy-start.2 = (s32[4]{0:T(128)S(1)}, s32[4]{0:T(128)}, u32[]{:S(2)}) copy-start(s32[4]{0:T(128)} %param.14) | copy-start | bytes 52
  128.0 219.5 %all-gather.8.cloned.1.call-start = ((), (), s32[]{:S(2)}) async-start(), calls=%async_computation.3 | async-start | bytes 17825792 | tf_op jit(solution)/shard_map/all_gather | solution.py:50
Sparse Core Ops, SparseCore 0:
  10.2 53.2 all-gather.3
  65.6 49.0 all-gather.5
  128.1 85.3 all-reduce.1
  215.5 131.9 all-gather.7
where the time goes:
time: 372 us
  waiting for transfers between devices  309 us (83%)
  matrix products  48 us (13%)
  between operations  13.8 us (4%)
    all_gather x1, waiting for transfers between devices, on_device(): every_query = lax.all_gather(query_features, 'tensor', axis=1, tiled=True)  132 us
    psum x1, waiting for transfers between devices, on_device(): full_g = lax.psum(part_g, 'tensor')  81 us
    all_gather x1, waiting for transfers between devices, on_device(): lax.all_gather(tokens, 'tensor', axis=0, tiled=True)  54.7 us
    all_gather x1, waiting for transfers between devices, on_device(): lax.all_gather(out_grad, 'tensor', axis=0, tiled=True)  39 us
    dot_general x1, matrix products, pair_scores(): lax.dot_general(feats, queries, (((1,), (1,)), ((), ())), precision=lax.P...  17.7 us
    dot_general x1, matrix products, on_device(): part_g = jnp.dot(grad_up, proj_out, preferred_element_type=jnp.float32)  13.2 us
    dot_general x1, matrix products, on_device(): gate = jnp.dot(whole_x, gate_weight, preferred_element_type=jnp.float32)  12.3 us
  transfers between devices with their start and end apart: 4, of which 4 were waited for; matrix products, arithmetic and copies ran while one was open for 5% of the time, Pallas kernels for 0%

commit v1 on v0

v1 whole, which is shorter than its diff:
```python
import functools

import jax
import jax.numpy as jnp
from jax import lax
from jax.experimental import pallas as pl
from jax.experimental.pallas import tpu as pltpu
from jax.sharding import PartitionSpec as P

F32 = jnp.float32
BF16 = jnp.bfloat16
CHUNK = 1024
LAG = 1
TILE = 256


def nt(a, b, precision=None):
    return lax.dot_general(
        a, b, (((1,), (1,)), ((), ())), precision=precision, preferred_element_type=F32
    )


def kernel(
    n, tok, dy, wg, wd, pin, pout, lens, q, feats_ref, scores_ref,
    buf, wgv, wdv, gate, hidden, pinv, poutv, qv, px, wt, fpart, frecv, spart, srecv, zrecv,
    own_sem, wg_sem, wd_sem, misc_sem, up_sem, dn_sem, ys_sem, cs_sem, zr_sem, yr_sem, cr_sem,
    fs_sem, fr_sem, ss_sem, sr_sem, zs_sem, zrr_sem,
):
    me = lax.axis_index("tensor")
    rows = tok.shape[0]
    lines = n // 4
    c = lax.rem(me, 2)
    y = lax.rem(me // 2, 2)
    z = me // 4
    jobs = buf.shape[0]
    half = jobs // 2
    total = buf.shape[1]
    examples = lens.shape[0]

    def index(zz, yy, cc):
        return (zz * 2 + yy) * 2 + cc

    def row(cc, yy, zz):
        return pl.multiple_of(((cc * 2 + yy) * lines + zz) * rows, rows)

    def own_copy(src, k, j):
        return pltpu.make_async_copy(
            src.at[:, pl.ds(pl.multiple_of(k * CHUNK, CHUNK), CHUNK)],
            buf.at[j, pl.ds(row(c, y, z), rows)], own_sem.at[j])

    def wg_copy(k):
        return pltpu.make_async_copy(
            wg.at[pl.ds(pl.multiple_of(k * CHUNK, CHUNK), CHUNK)], wgv.at[k], wg_sem.at[k])

    def wd_copy(k):
        return pltpu.make_async_copy(
            wd.at[:, pl.ds(pl.multiple_of(k * CHUNK, CHUNK), CHUNK)], wdv.at[k], wd_sem.at[k])

    small = [
        pltpu.make_async_copy(pin, pinv, misc_sem.at[0]),
        pltpu.make_async_copy(pout, poutv, misc_sem.at[1]),
        pltpu.make_async_copy(q, qv, misc_sem.at[2]),
    ]

    @pl.loop(0, half)
    def _(k):
        own_copy(tok, k, k).start()
        own_copy(dy, k, k + half).start()

    small[0].start()

    @pl.loop(0, half)
    def _(k):
        wg_copy(k).start()

    @pl.loop(0, half)
    def _(k):
        wd_copy(k).start()

    small[1].start()
    small[2].start()

    barrier = pltpu.get_barrier_semaphore()
    for i in range(1, n):
        pl.semaphore_signal(barrier, inc=1, device_id={"tensor": lax.rem(me + i, n)})
    pl.semaphore_wait(barrier, n - 1)

    gate[...] = jnp.zeros_like(gate)
    hidden[...] = jnp.zeros_like(hidden)
    px[...] = jnp.zeros_like(px)

    def block(j, start, size, send, recv, device):
        part = buf.at[j, pl.ds(start, size)]
        return pltpu.make_async_remote_copy(
            src_ref=part, dst_ref=part, send_sem=send, recv_sem=recv,
            device_id={"tensor": device})

    def up(j, o):
        return block(j, row(c, y, o), rows, up_sem.at[j], zr_sem.at[j, o], index(z + 1, y, c))

    def down(j, o):
        return block(j, row(c, y, o), rows, dn_sem.at[j], zr_sem.at[j, o], index(z - 1, y, c))

    def across(j, o):
        return block(j, row(c, y, o), rows, ys_sem.at[j], yr_sem.at[j], index(z, 1 - y, c))

    def twin(j, which, yy):
        return block(
            j, row(c, yy, 0), rows * lines, cs_sem.at[j, which], cr_sem.at[j, which],
            index(z, y, 1 - c))

    def arrived(j, start, size, sem):
        part = buf.at[j, pl.ds(start, size)]
        pltpu.make_async_copy(part, part, sem).wait()

    def inside(j):
        return jnp.logical_and(j >= 0, j < jobs)

    def step(s, carry):
        @pl.when(s < jobs)
        def _():
            arrived(s, row(c, y, z), rows, own_sem.at[s])

            @pl.when(z < lines - 1)
            def _():
                up(s, z).start()

            @pl.when(z > 0)
            def _():
                down(s, z).start()

            across(s, z).start()

        for h in range(1, lines):
            j = s - h * LAG

            @pl.when(jnp.logical_and(inside(j), z >= h))
            def _():
                o = z - h
                arrived(j, row(c, y, o), rows, zr_sem.at[j, o])

                @pl.when(z < lines - 1)
                def _():
                    up(j, o).start()

                across(j, o).start()

            @pl.when(jnp.logical_and(inside(j), z + h < lines))
            def _():
                o = z + h
                arrived(j, row(c, y, o), rows, zr_sem.at[j, o])

                @pl.when(z > 0)
                def _():
                    down(j, o).start()

                across(j, o).start()

        j1 = s - (lines - 1) * LAG

        @pl.when(inside(j1))
        def _():
            twin(j1, 0, y).start()

        j2 = s - lines * LAG

        @pl.when(inside(j2))
        def _():
            arrived(j2, row(c, 1 - y, 0), rows * lines, yr_sem.at[j2])
            twin(j2, 1, 1 - y).start()

        j3 = s - (lines + 1) * LAG

        @pl.when(inside(j3))
        def _():
            arrived(j3, row(1 - c, y, 0), rows * lines, cr_sem.at[j3, 0])
            arrived(j3, row(1 - c, 1 - y, 0), rows * lines, cr_sem.at[j3, 1])

        @pl.when(jnp.logical_and(j3 >= 0, j3 < half))
        def _():
            wg_copy(j3).wait()

            @pl.when(j3 == 0)
            def _():
                small[0].wait()

            @pl.loop(0, gate.shape[0])
            def _(t):
                gate[t] += jnp.dot(
                    buf[j3], wgv[j3, :, pl.ds(pl.multiple_of(t * gate.shape[2], 128), gate.shape[2])],
                    preferred_element_type=F32)

            px[...] += jnp.dot(
                buf[j3], pinv[pl.ds(pl.multiple_of(j3 * CHUNK, CHUNK), CHUNK)],
                preferred_element_type=F32)

        @pl.when(jnp.logical_and(j3 >= half, j3 < jobs))
        def _():
            k = j3 - half
            wd_copy(k).wait()

            @pl.loop(0, hidden.shape[0])
            def _(t):
                hidden[t] += nt(
                    buf[j3], wdv[k, pl.ds(pl.multiple_of(t * gate.shape[2], 128), hidden.shape[2])])

            @pl.when(k == 0)
            def _():
                @pl.loop(0, gate.shape[0])
                def _(t):
                    g = gate[t]
                    gate[t] = g / (1.0 + jnp.exp(-g))

                weighted()

        return carry

    width = px.shape[1]
    each = fpart.shape[0] // n
    per = each // examples

    def weighted():
        r = lax.broadcasted_iota(jnp.int32, (fpart.shape[0], width), 0)
        col = lax.broadcasted_iota(jnp.int32, (fpart.shape[0], width), 1)
        pick = jnp.where(r // examples == col, 1.0, 0.0).astype(F32)
        spread = nt(pick, px[...], lax.Precision.HIGHEST)
        e = lax.rem(lax.broadcasted_iota(jnp.int32, spread.shape, 0), examples)
        at = lax.broadcasted_iota(jnp.int32, spread.shape, 1)
        piece = at // rows
        oz = lax.rem(piece, lines)
        oy = lax.rem(piece // lines, 2)
        oc = piece // (2 * lines)
        token = index(oz, oy, oc) * rows + lax.rem(at, rows)
        begin = jnp.int32(0)
        mask = jnp.zeros(spread.shape, F32)
        for i in range(examples):
            end = begin + lens[i]
            mine = (e == i) & (token >= begin) & (token < end)
            mask = mask + jnp.where(mine, 1.0, 0.0)
            begin = end
        wt[...] = spread * mask

    lax.fori_loop(0, jobs + (lines + 1) * LAG, step, 0)

    small[1].wait()
    part_g = jnp.zeros((total, width), F32)
    for t in range(gate.shape[0]):
        grad_up = (hidden[t] * gate[t]).astype(BF16)
        part_g += jnp.dot(
            grad_up, poutv[t * gate.shape[2]:(t + 1) * gate.shape[2]], preferred_element_type=F32)
    fpart[...] = jnp.dot(
        wt[...], part_g, precision=lax.Precision.HIGHEST, preferred_element_type=F32)

    def deal(i):
        d = lax.rem(me + i, n)
        return pltpu.make_async_remote_copy(
            src_ref=fpart.at[pl.ds(pl.multiple_of(d * each, each), each)],
            dst_ref=frecv.at[i - 1], send_sem=fs_sem.at[i - 1], recv_sem=fr_sem.at[i - 1],
            device_id={"tensor": d})

    for i in range(1, n):
        deal(i).start()
    small[2].wait()
    mine = fpart[pl.ds(pl.multiple_of(me * each, each), each)]
    for i in range(1, n):
        deal(i).wait_recv()
    for i in range(1, n):
        mine = mine + frecv[i - 1]
    for i in range(per):
        feats_ref[:, i * width:(i + 1) * width] = mine[i * examples:(i + 1) * examples]
    spart[0] = nt(feats_ref[...], qv[...], lax.Precision.HIGHEST)

    def plane(p):
        yy, cc = lax.rem(y + p // 2, 2), lax.rem(c + p % 2, 2)
        return pltpu.make_async_remote_copy(
            src_ref=spart.at[0], dst_ref=srecv.at[p - 1], send_sem=ss_sem.at[p - 1],
            recv_sem=sr_sem.at[p - 1], device_id={"tensor": index(z, yy, cc)})

    def along(p):
        return pltpu.make_async_remote_copy(
            src_ref=spart.at[1], dst_ref=zrecv.at[p - 1], send_sem=zs_sem.at[p - 1],
            recv_sem=zrr_sem.at[p - 1], device_id={"tensor": index(lax.rem(z + p, lines), y, c)})

    for p in range(1, 4):
        plane(p).start()
    acc = spart[0]
    for p in range(1, 4):
        plane(p).wait_recv()
        acc = acc + srecv[p - 1]
    spart[1] = acc
    for p in range(1, lines):
        along(p).start()

    @pl.loop(0, jobs)
    def _(j):
        for zz in range(lines):
            @pl.when(jnp.logical_and(z == zz, zz < lines - 1))
            def _():
                arrived(j, 0, rows * (zz + 1), up_sem.at[j])

            @pl.when(jnp.logical_and(z == zz, zz > 0))
            def _():
                arrived(j, 0, rows * (lines - zz), dn_sem.at[j])

        arrived(j, 0, rows * lines, ys_sem.at[j])
        arrived(j, 0, rows * lines, cs_sem.at[j, 0])
        arrived(j, 0, rows * lines, cs_sem.at[j, 1])

    for i in range(1, n):
        deal(i).wait_send()
    for p in range(1, 4):
        plane(p).wait_send()
    for p in range(1, lines):
        along(p).wait_recv()
        acc = acc + zrecv[p - 1]
    for p in range(1, lines):
        along(p).wait_send()
    scores_ref[...] = acc


def on_device(n, tokens, out_grad, gate_weight, down_weight, proj_in, proj_out, lengths, queries):
    rows, depth = tokens.shape
    hidden = gate_weight.shape[1]
    width = proj_in.shape[1]
    count, columns = queries.shape
    examples = lengths.shape[0]
    total = rows * n
    half = depth // CHUNK
    jobs = 2 * half
    tile = TILE if hidden % TILE == 0 else 128
    tiles = hidden // tile
    lines = n // 4
    dma = pltpu.SemaphoreType.DMA
    anywhere = pl.BlockSpec(memory_space=pl.ANY)
    vmem = pl.BlockSpec(memory_space=pltpu.VMEM)
    smem = pl.BlockSpec(memory_space=pltpu.SMEM)
    feat_rows = examples * width
    return pl.pallas_call(
        functools.partial(kernel, n),
        out_shape=(
            jax.ShapeDtypeStruct((examples, columns), F32),
            jax.ShapeDtypeStruct((examples, count), F32),
        ),
        in_specs=[anywhere] * 6 + [smem, anywhere],
        out_specs=(vmem, vmem),
        scratch_shapes=[
            pltpu.VMEM((jobs, total, CHUNK), BF16),
            pltpu.VMEM((half, CHUNK, hidden), BF16),
            pltpu.VMEM((half, hidden, CHUNK), BF16),
            pltpu.VMEM((tiles, total, tile), F32),
            pltpu.VMEM((tiles, total, tile), F32),
            pltpu.VMEM((depth, width), BF16),
            pltpu.VMEM((hidden, width), BF16),
            pltpu.VMEM((count, columns), F32),
            pltpu.VMEM((total, width), F32),
            pltpu.VMEM((feat_rows, total), F32),
            pltpu.VMEM((feat_rows, width), F32),
            pltpu.VMEM((n - 1, feat_rows // n, width), F32),
            pltpu.VMEM((2, examples, count), F32),
            pltpu.VMEM((3, examples, count), F32),
            pltpu.VMEM((lines - 1, examples, count), F32),
            dma((jobs,)), dma((half,)), dma((half,)), dma((3,)),
            dma((jobs,)), dma((jobs,)), dma((jobs,)), dma((jobs, 2)),
            dma((jobs, lines)), dma((jobs,)), dma((jobs, 2)),
            dma((n - 1,)), dma((n - 1,)), dma((3,)), dma((3,)),
            dma((lines - 1,)), dma((lines - 1,)),
        ],
        compiler_params=pltpu.CompilerParams(
            collective_id=0, has_side_effects=True, vmem_limit_bytes=62 * 1024 * 1024
        ),
    )(tokens, out_grad, gate_weight, down_weight, proj_in, proj_out, lengths, queries)


def solution(mesh):
    placed = (
        P(("parts", "tensor"), None),
        P(("parts", "tensor"), None),
        P(None, "tensor"),
        P("tensor", None),
        P(),
        P("tensor", None),
        P("parts"),
        P(None, "tensor"),
    )
    return jax.shard_map(
        functools.partial(on_device, mesh.shape["tensor"]),
        mesh=mesh,
        in_specs=placed,
        out_specs=(P("parts", "tensor"), P("parts", None)),
        check_vma=False,
    )
```

time: 372 us -> 94.6 us (0.25)
  waiting for transfers between devices: 309 us -> 0 us
  Pallas kernels: 0 us -> 86.5 us
  matrix products: 48 us -> 0 us
  between operations: 13.8 us -> 0.64 us
  local copies, waits for them, and re-layouts: 0.73 us -> 7.21 us
    all_gather x3 -> x0, waiting for transfers between devices: 226 us -> none  [the longest x1 132 us: on_device(): every_query = lax.all_gather(query_features, 'tensor', axis=1, tiled=True)]
    pallas_call x0 -> x1, Pallas kernels: none -> 86.5 us  [on_device(): pl.pallas_call(functools.partial(kernel, n), out_shape=(jax.ShapeDtypeStr...]
    psum x1 -> x0, waiting for transfers between devices: 81 us -> none  [on_device(): full_g = lax.psum(part_g, 'tensor')]
    dot_general x5 -> x0, matrix products: 48 us -> none  [the longest x1 17.7 us: pair_scores(): lax.dot_general(feats, queries, (((1,), (1,)), ((), ())), precision=lax.P...]
    unnamed x6 -> x4, local copies, waits for them, and re-layouts: 0.02 us -> 7.21 us
  transfers between devices with their start and end apart: 4 -> 0, of which waited for: 4 -> 0; matrix products, arithmetic and copies ran while one was open for 5% -> 0% of each run, Pallas kernels for 0% -> 0%
where the time goes in v1:
time: 94.6 us; the launch traced here: 94.3 us
  Pallas kernels  86.5 us (91%)
  local copies, waits for them, and re-layouts  7.21 us (8%)
    pallas_call x1, Pallas kernels, on_device(): pl.pallas_call(functools.partial(kernel, n), out_shape=(jax.ShapeDtypeStr...  86.5 us
    unnamed x4, local copies, waits for them, and re-layouts  7.21 us

profile of v1, /device:TPU:0, one launch (start us, length us, event | category | flops | bytes accessed | tf_op | source)
XLA Modules:
  0.0 94.3 jit_solution(13001486214966502140)
XLA Ops:
  0.6 1.8 %copy.11.pout = bf16[1280,64]{1,0:T(8,128)(2,1)} copy(bf16[1280,64]{0,1:T(8,128)(2,1)} %param.13) | data formatting | bytes 327680 | tf_op args[5]
  2.5 2.8 %copy.10.pin = bf16[8192,64]{1,0:T(8,128)(2,1)} copy(bf16[8192,64]{0,1:T(8,128)(2,1)} %param.12) | data formatting | bytes 2097152 | tf_op args[4]
  5.3 86.5 %shard_map.95 = (f32[4,256]{1,0:T(4,128)}, f32[4,1024]{1,0:T(4,128)}) custom-call(bf16[16,8192]{1,0:T(8,128)(2,1)} %tok.1, bf16[16,8192]{1,0:T(8,128)(2,1)} %dy.1, bf16[8192,1280]{1,0:T(8,128)(2,1)} %wg.1, bf16[1280,8192]{1,0:T(8,128)(2,1)} %wd.1, bf16[8192,64]{1,0:T(8,128)(2,1)} %copy.10.pin, bf16[1280,64]{1,0:T(8,128)(2,1)} %copy.11.pout, s32[4]{0:T(128)} %lens.1, ...), custom_call_target="tpu_custom_call" | custom-call | tf_op jit(solution)/shard_map/pallas_call | solution.py:338
  91.7 1.3 %copy.14 = f32[4,256]{1,0:T(4,128)} copy(f32[4,256]{1,0:T(4,128)} %get-tuple-element.4) | data formatting | bytes 8192
  93.0 1.3 %copy.15 = f32[4,1024]{1,0:T(4,128)} copy(f32[4,1024]{1,0:T(4,128)} %get-tuple-element.5) | data formatting | bytes 32768

commit v2 on v1

--- a/solution.py
+++ b/solution.py
@@ -10,7 +10,7 @@
 F32 = jnp.float32
 BF16 = jnp.bfloat16
 CHUNK = 1024
-LAG = 1
+HOP, SIDE, TWIN = 2, 2, 1
 TILE = 256
 
 
@@ -95,11 +95,11 @@
             src_ref=part, dst_ref=part, send_sem=send, recv_sem=recv,
             device_id={"tensor": device})
 
-    def up(j, o):
-        return block(j, row(c, y, o), rows, up_sem.at[j], zr_sem.at[j, o], index(z + 1, y, c))
-
-    def down(j, o):
-        return block(j, row(c, y, o), rows, dn_sem.at[j], zr_sem.at[j, o], index(z - 1, y, c))
+    def up(j, o, yy):
+        return block(j, row(c, yy, o), rows, up_sem.at[j], zr_sem.at[j, o], index(z + 1, y, c))
+
+    def down(j, o, yy):
+        return block(j, row(c, yy, o), rows, dn_sem.at[j], zr_sem.at[j, o], index(z - 1, y, c))
 
     def across(j, o):
         return block(j, row(c, y, o), rows, ys_sem.at[j], yr_sem.at[j], index(z, 1 - y, c))
@@ -116,60 +116,82 @@
     def inside(j):
         return jnp.logical_and(j >= 0, j < jobs)
 
+    def across_first(j):
+        return lax.rem(j, 5) == 2
+
+    def both(a, b):
+        return jnp.logical_and(a, b)
+
+    def line_first(j):
+        return both(inside(j), jnp.logical_not(across_first(j)))
+
+    def pair_ready(j):
+        return both(inside(j), across_first(j))
+
+    def relay(j, o, ups, downs, sides):
+        if ups:
+            @pl.when(z < lines - 1)
+            def _():
+                for yy in sides:
+                    up(j, o, yy).start()
+        if downs:
+            @pl.when(z > 0)
+            def _():
+                for yy in sides:
+                    down(j, o, yy).start()
+
     def step(s, carry):
         @pl.when(s < jobs)
         def _():
             arrived(s, row(c, y, z), rows, own_sem.at[s])
-
-            @pl.when(z < lines - 1)
-            def _():
-                up(s, z).start()
-
-            @pl.when(z > 0)
-            def _():
-                down(s, z).start()
-
             across(s, z).start()
 
+        @pl.when(line_first(s))
+        def _():
+            relay(s, z, True, True, (y,))
+
+        p = s - SIDE
+
+        @pl.when(pair_ready(p))
+        def _():
+            arrived(p, row(c, 1 - y, z), rows, yr_sem.at[p])
+            relay(p, z, True, True, (y, 1 - y))
+
         for h in range(1, lines):
-            j = s - h * LAG
-
-            @pl.when(jnp.logical_and(inside(j), z >= h))
-            def _():
-                o = z - h
-                arrived(j, row(c, y, o), rows, zr_sem.at[j, o])
-
-                @pl.when(z < lines - 1)
-                def _():
-                    up(j, o).start()
-
-                across(j, o).start()
-
-            @pl.when(jnp.logical_and(inside(j), z + h < lines))
-            def _():
-                o = z + h
-                arrived(j, row(c, y, o), rows, zr_sem.at[j, o])
-
-                @pl.when(z > 0)
-                def _():
-                    down(j, o).start()
-
-                across(j, o).start()
-
-        j1 = s - (lines - 1) * LAG
-
-        @pl.when(inside(j1))
+            j = s - h * HOP
+            p = s - SIDE - h * HOP
+
+            for o, there, ups in ((z - h, z >= h, True), (z + h, z + h < lines, False)):
+                @pl.when(both(line_first(j), there))
+                def _(o=o, ups=ups, j=j):
+                    arrived(j, row(c, y, o), rows, zr_sem.at[j, o])
+                    relay(j, o, ups, not ups, (y,))
+                    across(j, o).start()
+
+                @pl.when(both(pair_ready(p), there))
+                def _(o=o, ups=ups, p=p):
+                    arrived(p, 0, rows * 2, zr_sem.at[p, o])
+                    relay(p, o, ups, not ups, (y, 1 - y))
+
+        j1 = s - (lines - 1) * HOP
+
+        @pl.when(line_first(j1))
         def _():
             twin(j1, 0, y).start()
 
-        j2 = s - lines * LAG
-
-        @pl.when(inside(j2))
+        j2 = j1 - SIDE
+
+        @pl.when(line_first(j2))
         def _():
             arrived(j2, row(c, 1 - y, 0), rows * lines, yr_sem.at[j2])
             twin(j2, 1, 1 - y).start()
 
-        j3 = s - (lines + 1) * LAG
+        @pl.when(pair_ready(j2))
+        def _():
+            twin(j2, 0, y).start()
+            twin(j2, 1, 1 - y).start()
+
+        j3 = j2 - TWIN
 
         @pl.when(inside(j3))
         def _():
@@ -190,9 +212,7 @@
                     buf[j3], wgv[j3, :, pl.ds(pl.multiple_of(t * gate.shape[2], 128), gate.shape[2])],
                     preferred_element_type=F32)
 
-            px[...] += jnp.dot(
-                buf[j3], pinv[pl.ds(pl.multiple_of(j3 * CHUNK, CHUNK), CHUNK)],
-                preferred_element_type=F32)
+            px[...] += nt(buf[j3], pinv[:, pl.ds(pl.multiple_of(j3 * CHUNK, CHUNK), CHUNK)])
 
         @pl.when(jnp.logical_and(j3 >= half, j3 < jobs))
         def _():
@@ -240,14 +260,13 @@
             begin = end
         wt[...] = spread * mask
 
-    lax.fori_loop(0, jobs + (lines + 1) * LAG, step, 0)
+    lax.fori_loop(0, jobs + (lines - 1) * HOP + SIDE + TWIN, step, 0)
 
     small[1].wait()
     part_g = jnp.zeros((total, width), F32)
     for t in range(gate.shape[0]):
         grad_up = (hidden[t] * gate[t]).astype(BF16)
-        part_g += jnp.dot(
-            grad_up, poutv[t * gate.shape[2]:(t + 1) * gate.shape[2]], preferred_element_type=F32)
+        part_g += nt(grad_up, poutv[:, t * gate.shape[2]:(t + 1) * gate.shape[2]])
     fpart[...] = jnp.dot(
         wt[...], part_g, precision=lax.Precision.HIGHEST, preferred_element_type=F32)
 
@@ -270,51 +289,42 @@
         feats_ref[:, i * width:(i + 1) * width] = mine[i * examples:(i + 1) * examples]
     spart[0] = nt(feats_ref[...], qv[...], lax.Precision.HIGHEST)
 
-    def plane(p):
-        yy, cc = lax.rem(y + p // 2, 2), lax.rem(c + p % 2, 2)
+    def tell(i):
         return pltpu.make_async_remote_copy(
-            src_ref=spart.at[0], dst_ref=srecv.at[p - 1], send_sem=ss_sem.at[p - 1],
-            recv_sem=sr_sem.at[p - 1], device_id={"tensor": index(z, yy, cc)})
-
-    def along(p):
-        return pltpu.make_async_remote_copy(
-            src_ref=spart.at[1], dst_ref=zrecv.at[p - 1], send_sem=zs_sem.at[p - 1],
-            recv_sem=zrr_sem.at[p - 1], device_id={"tensor": index(lax.rem(z + p, lines), y, c)})
-
-    for p in range(1, 4):
-        plane(p).start()
+            src_ref=spart.at[0], dst_ref=srecv.at[i - 1], send_sem=ss_sem.at[i - 1],
+            recv_sem=sr_sem.at[i - 1], device_id={"tensor": lax.rem(me + i, n)})
+
+    for i in range(1, n):
+        tell(i).start()
     acc = spart[0]
-    for p in range(1, 4):
-        plane(p).wait_recv()
-        acc = acc + srecv[p - 1]
-    spart[1] = acc
-    for p in range(1, lines):
-        along(p).start()
 
     @pl.loop(0, jobs)
     def _(j):
-        for zz in range(lines):
-            @pl.when(jnp.logical_and(z == zz, zz < lines - 1))
-            def _():
-                arrived(j, 0, rows * (zz + 1), up_sem.at[j])
-
-            @pl.when(jnp.logical_and(z == zz, zz > 0))
-            def _():
-                arrived(j, 0, rows * (lines - zz), dn_sem.at[j])
-
-        arrived(j, 0, rows * lines, ys_sem.at[j])
+        for width_of, test in ((1, line_first), (2, pair_ready)):
+            @pl.when(test(j))
+            def _(width_of=width_of):
+                for zz in range(lines):
+                    if zz < lines - 1:
+                        @pl.when(z == zz)
+                        def _(zz=zz):
+                            arrived(j, 0, rows * (zz + 1) * width_of, up_sem.at[j])
+                    if zz > 0:
+                        @pl.when(z == zz)
+                        def _(zz=zz):
+                            arrived(j, 0, rows * (lines - zz) * width_of, dn_sem.at[j])
+
+                arrived(j, 0, rows * (lines if width_of == 1 else 1), ys_sem.at[j])
+
         arrived(j, 0, rows * lines, cs_sem.at[j, 0])
         arrived(j, 0, rows * lines, cs_sem.at[j, 1])
 
     for i in range(1, n):
         deal(i).wait_send()
-    for p in range(1, 4):
-        plane(p).wait_send()
-    for p in range(1, lines):
-        along(p).wait_recv()
-        acc = acc + zrecv[p - 1]
-    for p in range(1, lines):
-        along(p).wait_send()
+    for i in range(1, n):
+        tell(i).wait_recv()
+        acc = acc + srecv[i - 1]
+    for i in range(1, n):
+        tell(i).wait_send()
     scores_ref[...] = acc
 
 
@@ -349,26 +359,26 @@
             pltpu.VMEM((half, hidden, CHUNK), BF16),
             pltpu.VMEM((tiles, total, tile), F32),
             pltpu.VMEM((tiles, total, tile), F32),
-            pltpu.VMEM((depth, width), BF16),
-            pltpu.VMEM((hidden, width), BF16),
+            pltpu.VMEM((width, depth), BF16),
+            pltpu.VMEM((width, hidden), BF16),
             pltpu.VMEM((count, columns), F32),
             pltpu.VMEM((total, width), F32),
             pltpu.VMEM((feat_rows, total), F32),
             pltpu.VMEM((feat_rows, width), F32),
             pltpu.VMEM((n - 1, feat_rows // n, width), F32),
             pltpu.VMEM((2, examples, count), F32),
-            pltpu.VMEM((3, examples, count), F32),
+            pltpu.VMEM((n - 1, examples, count), F32),
             pltpu.VMEM((lines - 1, examples, count), F32),
             dma((jobs,)), dma((half,)), dma((half,)), dma((3,)),
             dma((jobs,)), dma((jobs,)), dma((jobs,)), dma((jobs, 2)),
             dma((jobs, lines)), dma((jobs,)), dma((jobs, 2)),
-            dma((n - 1,)), dma((n - 1,)), dma((3,)), dma((3,)),
+            dma((n - 1,)), dma((n - 1,)), dma((n - 1,)), dma((n - 1,)),
             dma((lines - 1,)), dma((lines - 1,)),
         ],
         compiler_params=pltpu.CompilerParams(
             collective_id=0, has_side_effects=True, vmem_limit_bytes=62 * 1024 * 1024
         ),
-    )(tokens, out_grad, gate_weight, down_weight, proj_in, proj_out, lengths, queries)
+    )(tokens, out_grad, gate_weight, down_weight, proj_in.T, proj_out.T, lengths, queries)
 
 
 def solution(mesh):

time: 94.6 us -> 80.6 us (0.85)
  Pallas kernels: 86.5 us -> 76.5 us
  local copies, waits for them, and re-layouts: 7.21 us -> 2.59 us
    pallas_call x1, Pallas kernels: 86.5 us -> 76.5 us  [on_device(): pl.pallas_call(functools.partial(kernel, n), out_shape=(jax.ShapeDtypeStr...]
    unnamed x4 -> x2, local copies, waits for them, and re-layouts: 7.21 us -> 2.59 us
where the time goes in v2:
time: 80.6 us; the launch traced here: 79.7 us
  Pallas kernels  76.5 us (95%)
  local copies, waits for them, and re-layouts  2.59 us (3%)
    pallas_call x1, Pallas kernels, on_device(): pl.pallas_call(functools.partial(kernel, n), out_shape=(jax.ShapeDtypeStr...  76.5 us
    unnamed x2, local copies, waits for them, and re-layouts  2.59 us

profile of v2, /device:TPU:0, one launch (start us, length us, event | category | flops | bytes accessed | tf_op | source)
XLA Modules:
  0.0 79.7 jit_solution(11496128189006811217)
XLA Ops:
  0.6 76.5 %shard_map.95 = (f32[4,256]{1,0:T(4,128)}, f32[4,1024]{1,0:T(4,128)}) custom-call(bf16[16,8192]{1,0:T(8,128)(2,1)} %tok.1, bf16[16,8192]{1,0:T(8,128)(2,1)} %dy.1, bf16[8192,1280]{1,0:T(8,128)(2,1)} %wg.1, bf16[1280,8192]{1,0:T(8,128)(2,1)} %wd.1, bf16[64,8192]{1,0:T(8,128)(2,1)} %bitcast.2, bf16[64,1280]{1,0:T(8,128)(2,1)} %bitcast.3, s32[4]{0:T(128)} %lens.1, ...), custom_call_target="tpu_custom_call" | custom-call | tf_op jit(solution)/shard_map/pallas_call | solution.py:348
  77.1 1.3 %copy.12 = f32[4,256]{1,0:T(4,128)} copy(f32[4,256]{1,0:T(4,128)} %get-tuple-element.4) | data formatting | bytes 8192
  78.4 1.3 %copy.13 = f32[4,1024]{1,0:T(4,128)} copy(f32[4,1024]{1,0:T(4,128)} %get-tuple-element.5) | data formatting | bytes 32768

commit v3 on v2

--- a/solution.py
+++ b/solution.py
@@ -11,7 +11,7 @@
 BF16 = jnp.bfloat16
 CHUNK = 1024
 HOP, SIDE, TWIN = 2, 2, 1
-TILE = 256
+TILE = 1280
 
 
 def nt(a, b, precision=None):
@@ -43,6 +43,10 @@
     def row(cc, yy, zz):
         return pl.multiple_of(((cc * 2 + yy) * lines + zz) * rows, rows)
 
+    barrier = pltpu.get_barrier_semaphore()
+    for i in range(1, n):
+        pl.semaphore_signal(barrier, inc=1, device_id={"tensor": lax.rem(me + i, n)})
+
     def own_copy(src, k, j):
         return pltpu.make_async_copy(
             src.at[:, pl.ds(pl.multiple_of(k * CHUNK, CHUNK), CHUNK)],
@@ -80,14 +84,11 @@
     small[1].start()
     small[2].start()
 
-    barrier = pltpu.get_barrier_semaphore()
-    for i in range(1, n):
-        pl.semaphore_signal(barrier, inc=1, device_id={"tensor": lax.rem(me + i, n)})
-    pl.semaphore_wait(barrier, n - 1)
-
     gate[...] = jnp.zeros_like(gate)
     hidden[...] = jnp.zeros_like(hidden)
     px[...] = jnp.zeros_like(px)
+
+    pl.semaphore_wait(barrier, n - 1)
 
     def block(j, start, size, send, recv, device):
         part = buf.at[j, pl.ds(start, size)]

time: 80.6 us -> 74.4 us (0.923)
  Pallas kernels: 76.5 us -> 70.5 us
    pallas_call x1, Pallas kernels: 76.5 us -> 70.5 us  [on_device(): pl.pallas_call(functools.partial(kernel, n), out_shape=(jax.ShapeDtypeStr...]
where the time goes in v3:
time: 74.4 us; the launch traced here: 73.7 us
  Pallas kernels  70.5 us (95%)
  local copies, waits for them, and re-layouts  2.59 us (3%)
    pallas_call x1, Pallas kernels, on_device(): pl.pallas_call(functools.partial(kernel, n), out_shape=(jax.ShapeDtypeStr...  70.5 us
    unnamed x2, local copies, waits for them, and re-layouts  2.59 us

profile of v3, /device:TPU:0, one launch (start us, length us, event | category | flops | bytes accessed | tf_op | source)
XLA Modules:
  0.0 73.7 jit_solution(6341808986547318938)
XLA Ops:
  0.6 70.5 %shard_map.95 = (f32[4,256]{1,0:T(4,128)}, f32[4,1024]{1,0:T(4,128)}) custom-call(bf16[16,8192]{1,0:T(8,128)(2,1)} %tok.1, bf16[16,8192]{1,0:T(8,128)(2,1)} %dy.1, bf16[8192,1280]{1,0:T(8,128)(2,1)} %wg.1, bf16[1280,8192]{1,0:T(8,128)(2,1)} %wd.1, bf16[64,8192]{1,0:T(8,128)(2,1)} %bitcast.2, bf16[64,1280]{1,0:T(8,128)(2,1)} %bitcast.3, s32[4]{0:T(128)} %lens.1, ...), custom_call_target="tpu_custom_call" | custom-call | tf_op jit(solution)/shard_map/pallas_call | solution.py:349
  71.1 1.3 %copy.12 = f32[4,256]{1,0:T(4,128)} copy(f32[4,256]{1,0:T(4,128)} %get-tuple-element.4) | data formatting | bytes 8192
  72.4 1.3 %copy.13 = f32[4,1024]{1,0:T(4,128)} copy(f32[4,1024]{1,0:T(4,128)} %get-tuple-element.5) | data formatting | bytes 32768
